TPU v7x, 256 devices: a whole 4x4x8 slice. The times are simulated.
256 devices in a mesh: dp: 32 (over z_hi, x, core), seq: 8 (over y, z_lo).
Axes of the slice: x: 4, y: 4, z: 8 (z_hi: 4, z_lo: 2; z = z_hi * 2 + z_lo), core: 2. Of those that a mesh axis runs over, the one named last changes fastest.
Arguments:
- queries: bfloat16 [32, 1024, 4096], P('dp', 'seq'), may hold values from -6 to 6
- saved_key_state: bfloat16 [32, 1024, 512], P('dp', 'seq'), may hold values from -6 to 6
- saved_value_state: bfloat16 [32, 1024, 512], P('dp', 'seq'), may hold values from -6 to 6
- attn_output: bfloat16 [32, 1024, 4096], P('dp', 'seq'), may hold values from -4 to 4
- grad_output: bfloat16 [32, 1024, 4096], P('dp', 'seq'), may hold values from -6 to 6
- log_denominator: float32 [32, 1024, 32], P('dp', 'seq')
- layer_input: bfloat16 [32, 1024, 5120], P('dp', 'seq'), may hold values from -6 to 6
- doc_lengths: int32 [32, 8], P('dp'), may hold values from 1 to 512, as said below
- image_tiles: int32 [32, 8], P('dp'), may hold values from 0 to 4, as said below
Outputs:
- grad_queries: bfloat16 [32, 1024, 4096], P('dp', 'seq')
- keys_gradient: bfloat16 [32, 1024, 512], P('dp', 'seq')
- values_gradient: bfloat16 [32, 1024, 512], P('dp', 'seq')
- grad_value_weight: float32 [5120, 512], P(('dp', 'seq'))
Inputs may be any that keep to these rules, and one draw needn't show every extreme that they name: `doc_lengths`: in every sequence the 8 lengths sum to 1024 and exactly one of them equals 512. `image_tiles`: every sequence has a document with 4 tiles.
All inputs are finite; a program needn't handle non-finite values.
Results may differ from a plain program's by a relative error of at most 0.0059.
Values may be sent and summed in bfloat16 or wider, within the bound.
A program may use at most 128 MiB of HBM per device.

v0:
```python
import jax
import jax.numpy as jnp
from jax import lax
from jax.sharding import PartitionSpec as P

HQ = 32
KEY_VALUE_HEADS = 4
HEAD_SIZE = 128
TILE_TOK = 32


def token_tables(doc_lengths, image_tiles, seq_length):
    doc_ends = jnp.cumsum(doc_lengths)
    doc_starts = doc_ends - doc_lengths
    image_ends = doc_starts + jnp.minimum(image_tiles * TILE_TOK, doc_lengths)
    positions = jnp.arange(seq_length, dtype=jnp.int32)
    doc_index = jnp.sum((positions[:, None] >= doc_ends[None, :]).astype(jnp.int32), axis=1)
    picked = doc_index[:, None] == jnp.arange(doc_lengths.shape[0], dtype=jnp.int32)[None, :]
    image_end = jnp.sum(jnp.where(picked, image_ends[None, :], 0), axis=1)
    return (doc_index, positions < image_end)


def on_device(
    queries,
    saved_key_state,
    saved_value_state,
    attn_output,
    grad_output,
    log_denominator,
    layer_input,
    doc_lengths,
    image_tiles,
):
    sequence_workers = lax.axis_size("seq")
    data_devices = lax.axis_size("dp")
    tokens_per_worker = queries.shape[1]
    seq_length = tokens_per_worker * sequence_workers
    heads_local = HQ // sequence_workers
    local_key_value = max(1, KEY_VALUE_HEADS // sequence_workers)
    repeat_key_value = max(1, sequence_workers // KEY_VALUE_HEADS)
    group_local = heads_local // local_key_value
    score_scale = HEAD_SIZE ** (-0.5)
    grad_seq = grad_output[0]

    def widen(state_arrays):
        divide_heads = state_arrays[0].reshape(tokens_per_worker, KEY_VALUE_HEADS, HEAD_SIZE)
        return jnp.repeat(divide_heads, repeat_key_value, axis=1).reshape(
            tokens_per_worker, KEY_VALUE_HEADS * repeat_key_value * HEAD_SIZE
        )

    key_wide = widen(saved_key_state)
    value_wide = widen(saved_value_state)
    query_heads, heads_of_key, heads_of_value, grad_heads, output_heads = (
        lax.all_to_all(queries[0], "seq", split_axis=1, concat_axis=0, tiled=True),
        lax.all_to_all(key_wide, "seq", split_axis=1, concat_axis=0, tiled=True),
        lax.all_to_all(value_wide, "seq", split_axis=1, concat_axis=0, tiled=True),
        lax.all_to_all(grad_seq, "seq", split_axis=1, concat_axis=0, tiled=True),
        lax.all_to_all(attn_output[0], "seq", split_axis=1, concat_axis=0, tiled=True),
    )
    stat_heads = lax.all_to_all(log_denominator[0], "seq", split_axis=1, concat_axis=0, tiled=True)
    delta_heads = jnp.sum(
        (grad_heads.astype(jnp.float32) * output_heads.astype(jnp.float32)).reshape(
            seq_length, heads_local, HEAD_SIZE
        ),
        axis=2,
    )
    query_blocks = query_heads.reshape(seq_length, local_key_value, group_local, HEAD_SIZE)
    grad_blocks = grad_heads.reshape(seq_length, local_key_value, group_local, HEAD_SIZE)
    key_blocks = heads_of_key.reshape(seq_length, local_key_value, HEAD_SIZE)
    value_blocks = heads_of_value.reshape(seq_length, local_key_value, HEAD_SIZE)
    stat_blocks = stat_heads.reshape(seq_length, local_key_value, group_local)
    delta_blocks = delta_heads.reshape(seq_length, local_key_value, group_local)
    doc_index, image_flag = token_tables(doc_lengths[0], image_tiles[0], seq_length)
    row_block = min(512, seq_length)
    col_block = min(256, seq_length)
    col_count = seq_length // col_block
    tile_total = seq_length // row_block * col_count

    def tile_grads(running, row_start, col_start, visible):
        query_total, key_total, value_total = running
        query_tile = lax.dynamic_slice_in_dim(query_blocks, row_start, row_block, 0)
        grad_tile = lax.dynamic_slice_in_dim(grad_blocks, row_start, row_block, 0)
        stat_tile = jnp.transpose(
            lax.dynamic_slice_in_dim(stat_blocks, row_start, row_block, 0), (1, 2, 0)
        )
        delta_tile = jnp.transpose(
            lax.dynamic_slice_in_dim(delta_blocks, row_start, row_block, 0), (1, 2, 0)
        )
        key_tile = lax.dynamic_slice_in_dim(key_blocks, col_start, col_block, 0)
        value_tile = lax.dynamic_slice_in_dim(value_blocks, col_start, col_block, 0)
        scores = (
            jnp.einsum("qhgd,khd->hgqk", query_tile, key_tile, preferred_element_type=jnp.float32)
            * score_scale
        )
        attn_probs = jnp.where(visible[None, None], jnp.exp(scores - stat_tile[..., None]), 0.0)
        grad_probs = jnp.einsum(
            "qhgd,khd->hgqk", grad_tile, value_tile, preferred_element_type=jnp.float32
        )
        grad_scores = attn_probs * (grad_probs - delta_tile[..., None])
        probs_bf = attn_probs.astype(jnp.bfloat16)
        scores_bf = grad_scores.astype(jnp.bfloat16)
        query_part = (
            jnp.einsum("hgqk,khd->qhgd", scores_bf, key_tile, preferred_element_type=jnp.float32)
            * score_scale
        )
        key_part = (
            jnp.einsum("hgqk,qhgd->khd", scores_bf, query_tile, preferred_element_type=jnp.float32)
            * score_scale
        )
        value_part = jnp.einsum(
            "hgqk,qhgd->khd", probs_bf, grad_tile, preferred_element_type=jnp.float32
        )
        query_total = lax.dynamic_update_slice_in_dim(
            query_total,
            lax.dynamic_slice_in_dim(query_total, row_start, row_block, 0) + query_part,
            row_start,
            0,
        )
        key_total = lax.dynamic_update_slice_in_dim(
            key_total,
            lax.dynamic_slice_in_dim(key_total, col_start, col_block, 0) + key_part,
            col_start,
            0,
        )
        value_total = lax.dynamic_update_slice_in_dim(
            value_total,
            lax.dynamic_slice_in_dim(value_total, col_start, col_block, 0) + value_part,
            col_start,
            0,
        )
        return (query_total, key_total, value_total)

    def tile_step(tile_index, running):
        row_start = tile_index // col_count * row_block
        col_start = tile_index % col_count * col_block
        row_doc = lax.dynamic_slice_in_dim(doc_index, row_start, row_block, 0)
        col_doc = lax.dynamic_slice_in_dim(doc_index, col_start, col_block, 0)
        row_image = lax.dynamic_slice_in_dim(image_flag, row_start, row_block, 0)
        col_image = lax.dynamic_slice_in_dim(image_flag, col_start, col_block, 0)
        row_pos = row_start + jnp.arange(row_block, dtype=jnp.int32)
        col_pos = col_start + jnp.arange(col_block, dtype=jnp.int32)
        visible = (row_doc[:, None] == col_doc[None, :]) & (
            (col_pos[None, :] <= row_pos[:, None]) | row_image[:, None] & col_image[None, :]
        )
        updated = tile_grads(running, row_start, col_start, visible)
        return updated

    initial = (
        jnp.zeros((seq_length, local_key_value, group_local, HEAD_SIZE), jnp.float32),
        jnp.zeros((seq_length, local_key_value, HEAD_SIZE), jnp.float32),
        jnp.zeros((seq_length, local_key_value, HEAD_SIZE), jnp.float32),
    )
    query_total, key_total, value_total = lax.fori_loop(0, tile_total, tile_step, initial)
    query_grads = query_total.reshape(seq_length, heads_local * HEAD_SIZE).astype(jnp.bfloat16)
    grad_query_seq = lax.all_to_all(query_grads, "seq", split_axis=0, concat_axis=1, tiled=True)
    key_pieces, value_pieces = (
        lax.all_to_all(
            key_total.reshape(seq_length, local_key_value * HEAD_SIZE),
            "seq",
            split_axis=0,
            concat_axis=1,
            tiled=True,
        ),
        lax.all_to_all(
            value_total.reshape(seq_length, local_key_value * HEAD_SIZE),
            "seq",
            split_axis=0,
            concat_axis=1,
            tiled=True,
        ),
    )
    grad_key_seq = (
        jnp.sum(
            key_pieces.reshape(tokens_per_worker, KEY_VALUE_HEADS, repeat_key_value, HEAD_SIZE),
            axis=2,
        )
        .reshape(tokens_per_worker, KEY_VALUE_HEADS * HEAD_SIZE)
        .astype(jnp.bfloat16)
    )
    grad_value_seq = (
        jnp.sum(
            value_pieces.reshape(tokens_per_worker, KEY_VALUE_HEADS, repeat_key_value, HEAD_SIZE),
            axis=2,
        )
        .reshape(tokens_per_worker, KEY_VALUE_HEADS * HEAD_SIZE)
        .astype(jnp.bfloat16)
    )
    inputs_local = layer_input[0]
    total_tokens = tokens_per_worker * sequence_workers * data_devices
    own_rows = lax.psum_scatter(
        lax.dot_general(
            inputs_local,
            grad_value_seq,
            (((0,), (0,)), ((), ())),
            preferred_element_type=jnp.float32,
        ),
        ("dp", "seq"),
        scatter_dimension=0,
        tiled=True,
    )
    weight_rows = own_rows * total_tokens ** (-0.5)
    return (grad_query_seq[None], grad_key_seq[None], grad_value_seq[None], weight_rows)


def solution(mesh):
    return jax.shard_map(
        on_device,
        mesh=mesh,
        in_specs=(
            P("dp", "seq", None),
            P("dp", "seq", None),
            P("dp", "seq", None),
            P("dp", "seq", None),
            P("dp", "seq", None),
            P("dp", "seq", None),
            P("dp", "seq", None),
            P("dp", None),
            P("dp", None),
        ),
        out_specs=(
            P("dp", "seq", None),
            P("dp", "seq", None),
            P("dp", "seq", None),
            P(("dp", "seq"), None),
        ),
        check_vma=False,
    )
```

profile of v0, /device:TPU:32, one launch (start us, length us, event | category | flops | bytes accessed | tf_op | source)
XLA Modules:
  0.0 582.9 jit_solution(7555919121595306849)
XLA Ops:
  7.2 6.1 %all-to-all-start.2 = ((f32[128,8,4]{0,2,1:T(4,128)}), f32[128,8,4]{0,2,1:T(4,128)}, u32[]{:S(2)}, u32[]{:S(2)}) async-start(f32[128,8,4]{0,2,1:T(4,128)} %bitcast.205), calls=%async_computation.2 | async-start | bytes 32768 | tf_op jit(solution)/shard_map/all_to_all | solution.py:60
  14.2 3.9 all-to-all-done.2
  18.9 5.3 all-to-all-start
  25.6 4.9 all-to-all-done
  30.5 4.6 all-to-all-start.1
  36.4 11.0 %all-to-all-done.1 = bf16[128,8,512]{0,2,1:T(8,128)(2,1)S(1)} async-done(((bf16[128,8,512]{0,2,1:T(8,128)(2,1)}), bf16[128,8,512]{0,2,1:T(8,128)(2,1)S(1)}, u32[]{:S(2)}, u32[]{:S(2)}) %all-to-all-start.1) | async-done | bytes 1048608 | tf_op jit(solution)/shard_map/all_to_all | solution.py:54
  47.4 4.7 all-to-all-start.4
  52.1 2.3 copy.103
  54.4 9.0 %all-to-all-done.4 = bf16[128,8,512]{0,2,1:T(8,128)(2,1)S(1)} async-done(((bf16[128,8,512]{0,2,1:T(8,128)(2,1)}), bf16[128,8,512]{0,2,1:T(8,128)(2,1)S(1)}, u32[]{:S(2)}, u32[]{:S(2)}) %all-to-all-start.4) | async-done | bytes 1048608 | tf_op jit(solution)/shard_map/all_to_all | solution.py:57
  63.5 5.4 all-to-all-start.5
  72.1 7.3 %all-to-all-done.5 = bf16[128,8,512]{0,2,1:T(8,128)(2,1)} async-done(((bf16[128,8,512]{0,2,1:T(8,128)(2,1)}), bf16[128,8,512]{0,2,1:T(8,128)(2,1)}, u32[]{:S(2)}, u32[]{:S(2)}) %all-to-all-start.5) | async-done | bytes 1048608 | tf_op jit(solution)/shard_map/all_to_all | solution.py:58
  80.1 5.8 all-to-all-start.3
  88.2 2.3 reshape.349
  95.1 2.5 copy.104
  97.6 2.7 mul.97
  105.3 165.7 %while.19 = (s32[]{:T(128)}, f32[1024,1,4,128]{0,3,2,1:T(8,128)}, f32[1024,1,128]{2,0,1:T(8,128)}, f32[1024,1,128]{2,0,1:T(8,128)}, bf16[1024,1,128]{2,0,1:T(8,1...) while((s32[]{:T(128)}, f32[1024,1,4,128]{0,3,2,1:T(8,128)}, ...), condition=%wide.region_5.6_spmd, body=%wide.region_4.5_spmd.sunk | while | flops 676037376 | bytes 41944880 | solution.py:153
  264.2 2.2 fusion.67
  272.3 13.0 %all_to_all.138 = f32[8,128,128]{1,2,0:T(8,128)S(1)} all-to-all(f32[8,128,128]{1,2,0:T(8,128)S(1)} %copy.114), channel_id=1, replica_groups=mesh['dp'=32,'seq'=8] {'seq'}, dimensions={0} | all-to-all | bytes 1048576 | tf_op jit(solution)/shard_map/all_to_all | solution.py:164
  285.4 5.3 convolution_bitcast_fusion.2
  292.9 5.2 all-to-all-start.7
  300.0 6.6 %all-to-all-done.7 = f32[8,128,128]{1,2,0:T(8,128)} async-done(((f32[8,128,128]{1,2,0:T(8,128)}), f32[8,128,128]{1,2,0:T(8,128)}, u32[]{:S(2)}, u32[]{:S(2)}) %all-to-all-start.7) | async-done | bytes 524320 | tf_op jit(solution)/shard_map/all_to_all | solution.py:157
  306.6 5.0 all-to-all-start.6
  314.2 9.3 %all-to-all-done.6 = bf16[8,128,512]{2,1,0:T(8,128)(2,1)S(1)} async-done(((bf16[8,128,512]{2,1,0:T(8,128)(2,1)}), bf16[8,128,512]{2,1,0:T(8,128)(2,1)S(1)}, u32[]{:S(2)}, u32[]{:S(2)}) %all-to-all-start.6) | async-done | bytes 1048608 | tf_op jit(solution)/shard_map/all_to_all | solution.py:155
  325.5 248.7 %all-reduce.3.cloned.1.call-done = f32[5120,512]{0,1:T(8,128)} async-done(((f32[5120,512]{0,1:T(8,128)}), f32[5120,512]{0,1:T(8,128)}) %all-reduce.3.cloned.1.call-update) | async-done | bytes 10485776
  (258 shorter events, 194.7 us)
Async XLA Ops:
  7.2 278.2 %copy-start = (bf16[1,128,5120]{2,1,0:T(8,128)(2,1)S(1)}, bf16[1,128,5120]{2,1,0:T(8,128)(2,1)}, u32[]{:S(2)}) copy-start(bf16[1,128,5120]{2,1,0:T(8,128)(2,1)} %param.17) | copy-start | bytes 3932164
  7.2 17.1 %copy-start.5 = (bf16[1,128,4096]{2,1,0:T(8,128)(2,1)S(1)}, bf16[1,128,4096]{2,1,0:T(8,128)(2,1)}, u32[]{:S(2)}) copy-start(bf16[1,128,4096]{2,1,0:T(8,128)(2,1)} %param.11) | copy-start | bytes 3145732
  7.2 11.0 %all-to-all-start.2 = ((f32[128,8,4]{0,2,1:T(4,128)}), f32[128,8,4]{0,2,1:T(4,128)}, u32[]{:S(2)}, u32[]{:S(2)}) async-start(f32[128,8,4]{0,2,1:T(4,128)} %bitcast.205), calls=%async_computation.2 | async-start | bytes 32768 | tf_op jit(solution)/shard_map/all_to_all | solution.py:60
  18.9 11.6 %all-to-all-start = ((bf16[128,8,128]{2,0,1:T(8,128)(2,1)}), bf16[128,8,128]{2,0,1:T(8,128)(2,1)}, u32[]{:S(2)}, u32[]{:S(2)}) async-start(bf16[128,8,128]{2,0,1:T(8,128)(2,1)} %bitcast.25), calls=%async_computation | async-start | bytes 524288 | tf_op jit(solution)/shard_map/all_to_all | solution.py:55
  24.2 10.9 %copy-start.6 = (bf16[1,128,4096]{2,1,0:T(8,128)(2,1)S(1)}, bf16[1,128,4096]{2,1,0:T(8,128)(2,1)}, u32[]{:S(2)}) copy-start(bf16[1,128,4096]{2,1,0:T(8,128)(2,1)} %param.15) | copy-start | bytes 3145732
  30.5 16.9 %all-to-all-start.1 = ((bf16[128,8,512]{0,2,1:T(8,128)(2,1)}), bf16[128,8,512]{0,2,1:T(8,128)(2,1)S(1)}, u32[]{:S(2)}, u32[]{:S(2)}) async-start(bf16[128,8,512]{0,2,1:T(8,128)(2,1)} %bitcast.32), calls=%async_computation.1 | async-start | bytes 2097152 | tf_op jit(solution)/shard_map/all_to_all | solution.py:54
  47.4 16.1 %all-to-all-start.4 = ((bf16[128,8,512]{0,2,1:T(8,128)(2,1)}), bf16[128,8,512]{0,2,1:T(8,128)(2,1)S(1)}, u32[]{:S(2)}, u32[]{:S(2)}) async-start(bf16[128,8,512]{0,2,1:T(8,128)(2,1)} %bitcast.197), calls=%async_computation.4 | async-start | bytes 2097152 | tf_op jit(solution)/shard_map/all_to_all | solution.py:57
  52.1 16.7 %copy-start.8 = (s32[1,8]{1,0:T(1,128)S(1)}, s32[1,8]{1,0:T(1,128)}, u32[]{:S(2)}) copy-start(s32[1,8]{1,0:T(1,128)} %param.18) | copy-start | bytes 100
  52.1 16.9 %copy-start.7 = (bf16[1,128,512]{2,1,0:T(8,128)(2,1)S(1)}, bf16[1,128,512]{2,1,0:T(8,128)(2,1)}, u32[]{:S(2)}) copy-start(bf16[1,128,512]{2,1,0:T(8,128)(2,1)} %param.13) | copy-start | bytes 393220
  52.1 19.2 %copy-start.9 = (s32[1,8]{1,0:T(1,128)S(1)}, s32[1,8]{1,0:T(1,128)}, u32[]{:S(2)}) copy-start(s32[1,8]{1,0:T(1,128)} %param.19) | copy-start | bytes 100
  63.5 15.9 %all-to-all-start.5 = ((bf16[128,8,512]{0,2,1:T(8,128)(2,1)}), bf16[128,8,512]{0,2,1:T(8,128)(2,1)}, u32[]{:S(2)}, u32[]{:S(2)}) async-start(bf16[128,8,512]{0,2,1:T(8,128)(2,1)} %bitcast.196), calls=%async_computation.5 | async-start | bytes 2097152 | tf_op jit(solution)/shard_map/all_to_all | solution.py:58
  80.1 22.0 %all-to-all-start.3 = ((bf16[128,8,128]{2,0,1:T(8,128)(2,1)}), bf16[128,8,128]{2,0,1:T(8,128)(2,1)}, u32[]{:S(2)}, u32[]{:S(2)}) async-start(bf16[128,8,128]{2,0,1:T(8,128)(2,1)} %bitcast.202), calls=%async_computation.3 | async-start | bytes 524288 | tf_op jit(solution)/shard_map/all_to_all | solution.py:56
  85.9 488.3 %all-reduce.3.cloned.1.call-start = ((), (), s32[]{:S(2)}) async-start(), calls=%async_computation.9 | async-start | bytes 20971520
  111.0 3.6 copy-start.1
  131.7 3.6 copy-start.1
  152.4 3.6 copy-start.1
  173.1 3.6 copy-start.1
  193.8 3.6 copy-start.1
  214.5 3.6 copy-start.1
  235.3 3.6 copy-start.1
  256.0 3.6 copy-start.1
  290.7 7.4 %copy-start.4 = (f32[1024,1,4,128]{0,3,2,1:T(8,128)S(1)}, f32[1024,1,4,128]{0,3,2,1:T(8,128)}, u32[]{:S(2)}) copy-start(f32[1024,1,4,128]{0,3,2,1:T(8,128)} %get-tuple-element.295) | copy-start | bytes 6291460
  292.9 13.7 %all-to-all-start.7 = ((f32[8,128,128]{1,2,0:T(8,128)}), f32[8,128,128]{1,2,0:T(8,128)}, u32[]{:S(2)}, u32[]{:S(2)}) async-start(f32[8,128,128]{1,2,0:T(8,128)} %copy.110), calls=%async_computation.7 | async-start | bytes 1048576 | tf_op jit(solution)/shard_map/all_to_all | solution.py:157
  306.6 16.9 %all-to-all-start.6 = ((bf16[8,128,512]{2,1,0:T(8,128)(2,1)}), bf16[8,128,512]{2,1,0:T(8,128)(2,1)S(1)}, u32[]{:S(2)}, u32[]{:S(2)}) async-start(bf16[8,128,512]{2,1,0:T(8,128)(2,1)} %copy.129), calls=%async_computation.6 | async-start | bytes 2097152 | tf_op jit(solution)/shard_map/all_to_all | solution.py:155
  (16 other events, 29.6 us)
Sparse Core Ops, SparseCore 0:
  290.9 283.2 all-reduce.2
where the time goes:
time: 589 us; the launch traced here: 583 us
  waiting for transfers between devices  301 us (51%)
  local copies, waits for them, and re-layouts  127 us (22%)
  matrix products  74.9 us (13%)
  starting transfers between devices  42.2 us (7%)
  between operations  14.2 us (2%)
  blocking collectives  13 us (2%)
  other arithmetic  9.67 us (2%)
    unnamed x2, waiting for transfers between devices  249 us
    dot_general x8, matrix products, tile_grads(): jnp.einsum('hgqk,qhgd->khd', scores_bf, query_tile, preferred_element_typ...  17.6 us
    while x48, local copies, waits for them, and re-layouts  17.5 us
    dot_general x8, matrix products, tile_grads(): jnp.einsum('hgqk,qhgd->khd', probs_bf, grad_tile, preferred_element_type=...  16.7 us
    dynamic_slice x16, local copies, waits for them, and re-layouts, tile_grads(): lax.dynamic_slice_in_dim(value_total, col_start, col_block, 0) + value_part  13.9 us
    dot_general x8, matrix products, tile_grads(): jnp.einsum('qhgd,khd->hgqk', query_tile, key_tile, preferred_element_type...  13.7 us
    dynamic_update_slice x16, local copies, waits for them, and re-layouts, tile_grads(): lax.dynamic_update_slice_in_dim(key_total, lax.dynamic_slice_in_dim(key_t...  13.3 us
    dynamic_slice x8, local copies, waits for them, and re-layouts, tile_grads(): lax.dynamic_slice_in_dim(key_total, col_start, col_block, 0) + key_part  13.3 us
  transfers between devices with their start and end apart: 9, of which 8 were waited for; matrix products, arithmetic and copies ran while one was open for 6% of the time, Pallas kernels for 0%

commit v1 on v0

v1 whole, which is shorter than its diff:
```python
import functools
import math

import jax
import jax.numpy as jnp
from jax import lax
from jax.experimental import pallas as pl
from jax.experimental.pallas import tpu as pltpu
from jax.sharding import PartitionSpec as P

HQ = 32
KV = 4
HEAD = 128
GROUP = HQ // KV
TILE_TOK = 32
TOK = 128
CORES = 2
SCALE = HEAD ** -0.5
LOG2E = math.log2(math.e)
HIDDEN = -1e30
REL = (0, 1, -1, -2, -3, -4)
NT = (((1,), (1,)), ((), ()))


def kernel(
    nx, nz, ns, doc_ref, tiles_ref, q_hbm, k_hbm, v_hbm, o_hbm, do_hbm, lse_hbm, x_hbm,
    dq_hbm, dk_hbm, dv_hbm, dw_hbm,
    q_s, o_s, do_s, lse_s, x_s, kvb, bias, lse_t, dq_s, own, sb, rb, dkv,
    x_t, xg, xp, dvall, wf, st1, r1, acc, st2, r2, out_s,
    ld_kv, ld, out_sem, kv_ss, kv_rs, pg_ss, pg_rs, x_ss, x_rs, ag_ss, ag_rs, rs_ss, rs_rs, z_ss, z_rs,
):
    nxc = nx * CORES
    d = lax.axis_index("dp")
    s = lax.axis_index("seq")
    zh = d // nxc
    i = lax.rem(d, nxc)
    xc = i // CORES
    core = lax.rem(i, CORES)
    rows = wf.shape[1]
    part = rows // ns
    own_rows = part // nz

    def remote(src, dst, ss, rs, **where):
        return pltpu.make_async_remote_copy(
            src_ref=src, dst_ref=dst, send_sem=ss, recv_sem=rs, device_id=where,
            device_id_type=pl.DeviceIdType.MESH,
        )

    def inside(t):
        return (t >= 0) & (t < ns)

    def wrap(t):
        return lax.rem(t + ns, ns)

    for g in range(KV):
        pltpu.make_async_copy(k_hbm.at[:, pl.ds(g * HEAD, HEAD)], kvb.at[0, g, 0], ld_kv.at[g, 0]).start()
        pltpu.make_async_copy(v_hbm.at[:, pl.ds(g * HEAD, HEAD)], kvb.at[0, g, 1], ld_kv.at[g, 1]).start()
    loads = [
        pltpu.make_async_copy(src, dst, ld.at[n])
        for n, (src, dst) in enumerate(
            ((x_hbm, x_s), (do_hbm, do_s), (o_hbm, o_s), (q_hbm, q_s), (lse_hbm, lse_s))
        )
    ]
    for copy in loads:
        copy.start()
    for c in range(1, len(REL)):
        @pl.when(jnp.logical_not(inside(s + REL[c])))
        def _():
            kvb[c] = jnp.zeros(kvb.shape[1:], kvb.dtype)

    barrier = pltpu.get_barrier_semaphore()
    peers = [dict(seq=wrap(s + m)) for m in range(1, ns)]
    peers += [dict(dp=zh * nxc + lax.rem(i + m, nxc)) for m in range(1, nxc)]
    peers += [dict(dp=lax.rem(zh + m, nz) * nxc + i) for m in range(1, nz)]
    for peer in peers:
        pl.semaphore_signal(barrier, inc=1, device_id=peer, device_id_type=pl.DeviceIdType.MESH)
    pl.semaphore_wait(barrier, len(peers))

    def kv_copy(g, c):
        return remote(
            kvb.at[0, g], kvb.at[c, g], kv_ss.at[c - 1, g], kv_rs.at[c - 1, g], seq=wrap(s - REL[c])
        )

    def pg_copy(g, c):
        return remote(
            sb.at[c - 1, g], rb.at[c - 1, g], pg_ss.at[c - 1, g], pg_rs.at[c - 1, g], seq=wrap(s + REL[c])
        )

    for g in range(KV):
        for half in range(2):
            src = (k_hbm, v_hbm)[half]
            pltpu.make_async_copy(src.at[:, pl.ds(g * HEAD, HEAD)], kvb.at[0, g, half], ld_kv.at[g, half]).wait()
        for c in range(1, len(REL)):
            @pl.when(inside(s - REL[c]))
            def _():
                kv_copy(g, c).start()

    loads[0].wait()
    slab = rows // nz
    for tile in range(x_s.shape[1] // TOK):
        turned = x_s[:, tile * TOK:(tile + 1) * TOK].T
        at = tile * TOK
        while at < (tile + 1) * TOK:
            block, offset = divmod(at, slab)
            length = min((tile + 1) * TOK - at, slab - offset)
            lead = at - tile * TOK
            x_t[block // nxc, block % nxc, offset:offset + length, :] = turned[lead:lead + length, :]
            at += length

    def x_copy(m):
        j = lax.rem(i + m, nxc)
        return remote(x_t.at[:, j], xg.at[i], x_ss.at[m - 1], x_rs.at[m - 1], dp=zh * nxc + j)

    for m in range(1, nxc):
        x_copy(m).start()
    xg[i] = x_t[:, i]

    row = s * TOK + lax.broadcasted_iota(jnp.int32, (1, TOK), 1)
    low = jnp.zeros((1, TOK), jnp.int32)
    high = jnp.zeros((1, TOK), jnp.int32)
    start = jnp.int32(0)
    for n in range(doc_ref.shape[1]):
        length = doc_ref[0, n]
        image_end = start + jnp.minimum(tiles_ref[0, n] * TILE_TOK, length)
        here = row >= start
        low = jnp.where(here, start, low)
        high = jnp.where(here, image_end, high)
        start = start + length
    high = jnp.maximum(row + 1, high)
    for c in range(len(REL)):
        key = (s + REL[c]) * TOK + lax.broadcasted_iota(jnp.int32, (TOK, TOK), 0)
        tile = jnp.where((key >= low) & (key < high), 0.0, HIDDEN).astype(jnp.float32)
        p, half = divmod(c, 2)
        bias[p, half * TOK:(half + 1) * TOK, :TOK] = tile
        bias[p, half * TOK:(half + 1) * TOK, TOK:] = tile
    loads[4].wait()
    lse_t[...] = lse_s[...].T * LOG2E
    for copy in loads[1:4]:
        copy.wait()

    head_lane = lax.broadcasted_iota(jnp.int32, (GROUP, GROUP * HEAD), 1)
    head_row = lax.broadcasted_iota(jnp.int32, (GROUP, GROUP * HEAD), 0)
    picks = ((head_lane >= head_row * HEAD) & (head_lane < (head_row + 1) * HEAD)).astype(jnp.bfloat16)

    def dq_copy(g):
        cols = pl.ds(g * GROUP * HEAD, GROUP * HEAD)
        return pltpu.make_async_copy(dq_s.at[:, cols], dq_hbm.at[:, cols], out_sem.at[g])

    def attend(g, carry):
        base = g * GROUP * HEAD

        def heads(ref):
            return jnp.concatenate([ref[:, pl.ds(base + h * HEAD, HEAD)] for h in range(GROUP)], axis=0)

        wide = pl.ds(base, GROUP * HEAD)
        product = do_s[:, wide].astype(jnp.float32) * o_s[:, wide].astype(jnp.float32)
        coarse = product.astype(jnp.bfloat16)
        fine = (product - coarse.astype(jnp.float32)).astype(jnp.bfloat16)
        delta = lax.dot_general(picks, coarse, NT, preferred_element_type=jnp.float32)
        delta += lax.dot_general(picks, fine, NT, preferred_element_type=jnp.float32)
        stat = lse_t[pl.ds(pl.multiple_of(g * GROUP, GROUP), GROUP), :]
        q8, do8 = heads(q_s), heads(do_s)
        total = None
        for p in range(len(REL) // 2):
            for c in (2 * p, 2 * p + 1):
                if c:
                    @pl.when(inside(s + REL[c]))
                    def _():
                        kv_copy(g, c).wait_recv()
            keys = jnp.concatenate([kvb[2 * p, g, 0], kvb[2 * p + 1, g, 0]], axis=0)
            values = jnp.concatenate([kvb[2 * p, g, 1], kvb[2 * p + 1, g, 1]], axis=0)
            probs, steps = [], []
            for pair in range(GROUP // 2):
                cut = slice(pair * 2 * TOK, (pair + 1) * 2 * TOK)
                two = [pair * 2, pair * 2 + 1]
                stat_row = jnp.concatenate([stat[h:h + 1] for h in two], axis=1)
                delta_row = jnp.concatenate([delta[h:h + 1] for h in two], axis=1)
                scores = lax.dot_general(keys, q8[cut], NT, preferred_element_type=jnp.float32)
                prob = jnp.exp2(scores * (SCALE * LOG2E) - stat_row + bias[p])
                grad = lax.dot_general(values, do8[cut], NT, preferred_element_type=jnp.float32)
                probs.append(prob.astype(jnp.bfloat16))
                steps.append((prob * (grad - delta_row)).astype(jnp.bfloat16))
            probs = jnp.concatenate(probs, axis=1)
            steps = jnp.concatenate(steps, axis=1)
            dv = jnp.dot(probs, do8, preferred_element_type=jnp.float32)
            dk = jnp.dot(steps, q8, preferred_element_type=jnp.float32) * SCALE
            dq = jnp.dot(keys.T, steps, preferred_element_type=jnp.float32)
            total = dq if total is None else total + dq
            for c in (2 * p, 2 * p + 1):
                half = slice((c - 2 * p) * TOK, (c - 2 * p + 1) * TOK)
                if c == 0:
                    own[g, 0] = dk[half]
                    own[g, 1] = dv[half]
                else:
                    sb[c - 1, g, 0] = dk[half].astype(jnp.bfloat16)
                    sb[c - 1, g, 1] = dv[half].astype(jnp.bfloat16)

                    @pl.when(inside(s + REL[c]))
                    def _():
                        pg_copy(g, c).start()
        for h in range(GROUP):
            dq_s[:, pl.ds(base + h * HEAD, HEAD)] = (
                total[:, h * TOK:(h + 1) * TOK].T * SCALE
            ).astype(jnp.bfloat16)
        dq_copy(g).start()
        return carry

    lax.fori_loop(0, KV, attend, 0)

    old = lax.broadcasted_iota(jnp.int32, (1, rows), 1)
    new = old
    before = 0
    for n in range(1, nz * ns):
        shift = (n % ns * nz + n // ns - n) * own_rows
        new = new + jnp.where(old >= n * own_rows, shift - before, 0)
        before = shift
    order = (lax.broadcasted_iota(jnp.int32, (rows, rows), 0) == new).astype(jnp.bfloat16)
    for m in range(1, nxc):
        x_copy(m).wait_recv()

    def reorder(jj, carry):
        two = jnp.concatenate([xg[2 * jj].reshape(rows, TOK), xg[2 * jj + 1].reshape(rows, TOK)], axis=1)
        xp[:, pl.ds(pl.multiple_of(jj * 2 * TOK, 2 * TOK), 2 * TOK)] = jnp.dot(
            order, two, preferred_element_type=jnp.float32
        ).astype(jnp.bfloat16)
        return carry

    lax.fori_loop(0, nxc // 2, reorder, 0)

    def ag_copy(g, j, n, **where):
        return remote(dvall.at[g, j], dvall.at[g, j], ag_ss.at[g, n], ag_rs.at[g, j], **where)

    sibling = (zh * nx + xc) * CORES + 1 - core

    def along_x(m):
        return lax.rem(xc + m, nx)

    def settle(g, carry):
        for c in range(1, len(REL)):
            @pl.when(inside(s - REL[c]))
            def _():
                pg_copy(g, c).wait_recv()
                own[g] += rb[c - 1, g].astype(jnp.float32)
        done = own[g].astype(jnp.bfloat16)
        cols = pl.ds(pl.multiple_of(g * HEAD, HEAD), HEAD)
        dkv[0, :, cols] = done[0]
        dkv[1, :, cols] = done[1]
        dvall[g, i] = done[1]
        for m in range(1, nx):
            ag_copy(g, i, m - 1, dp=(zh * nx + along_x(m)) * CORES + core).start()
        ag_copy(g, i, nx - 1, dp=sibling).start()
        return carry

    lax.fori_loop(0, KV, settle, 0)
    out_k = pltpu.make_async_copy(dkv.at[0], dk_hbm, out_sem.at[KV])
    out_v = pltpu.make_async_copy(dkv.at[1], dv_hbm, out_sem.at[KV + 1])
    out_k.start()
    out_v.start()

    def relay(g, carry):
        for m in range(1, nx):
            j = along_x(m) * CORES + core
            ag_copy(g, j, nx - 1 + m, dp=sibling).wait_recv()
            ag_copy(g, j, nx - 1 + m, dp=sibling).start()
        return carry

    lax.fori_loop(0, KV, relay, 0)

    def rs_copy(g, m):
        to = wrap(s + m)
        return remote(st1.at[g, to], r1.at[g, m - 1], rs_ss.at[g, m - 1], rs_rs.at[g, m - 1], seq=to)

    def weight(g, carry):
        for m in range(nx):
            j = along_x(m) * CORES + 1 - core
            ag_copy(g, j, 0, dp=sibling).wait_recv()
        values = dvall[g].reshape(nxc * TOK, HEAD)
        product = jnp.dot(xp[...], values, preferred_element_type=jnp.float32)
        wf[g] = product
        st1[g] = product.astype(jnp.bfloat16).reshape(ns, part, HEAD)
        for m in range(1, ns):
            rs_copy(g, m).start()
        return carry

    lax.fori_loop(0, KV, weight, 0)

    st2[...] = jnp.zeros(st2.shape, st2.dtype)

    def gather_rows(g, carry):
        mine = wf[g, pl.ds(pl.multiple_of(s * part, part), part), :]
        for m in range(1, ns):
            rs_copy(g, m).wait_recv()
            mine = mine + r1[g, m - 1].astype(jnp.float32)
        acc[:, pl.ds(pl.multiple_of(g * HEAD, HEAD), HEAD)] = mine
        return carry

    lax.fori_loop(0, KV, gather_rows, 0)
    for n in range(nz):
        st2[n, :own_rows, :] = acc[n * own_rows:(n + 1) * own_rows, :]

    def z_copy(m):
        to = lax.rem(zh + m, nz)
        return remote(st2.at[to], r2.at[m - 1], z_ss.at[m - 1], z_rs.at[m - 1], dp=to * nxc + i)

    for m in range(1, nz):
        z_copy(m).start()
    result = st2[zh, :own_rows, :]
    for m in range(1, nz):
        z_copy(m).wait_recv()
        result = result + r2[m - 1, :own_rows, :]
    out_s[...] = result * ((ns * nz * nxc * TOK) ** -0.5)
    out_w = pltpu.make_async_copy(out_s, dw_hbm, out_sem.at[KV + 2])
    out_w.start()

    def drain(g, carry):
        for c in range(1, len(REL)):
            @pl.when(inside(s - REL[c]))
            def _():
                kv_copy(g, c).wait_send()

            @pl.when(inside(s + REL[c]))
            def _():
                pg_copy(g, c).wait_send()
        for m in range(1, nx):
            ag_copy(g, i, m - 1, dp=sibling).wait_send()
            ag_copy(g, i, nx - 1 + m, dp=sibling).wait_send()
        ag_copy(g, i, nx - 1, dp=sibling).wait_send()
        for m in range(1, ns):
            rs_copy(g, m).wait_send()
        dq_copy(g).wait()
        return carry

    lax.fori_loop(0, KV, drain, 0)
    for m in range(1, nxc):
        x_copy(m).wait_send()
    for m in range(1, nz):
        z_copy(m).wait_send()
    out_k.wait()
    out_v.wait()
    out_w.wait()


def solution(mesh, nx=4):
    ns = mesh.shape["seq"]
    nxc = nx * CORES
    nz = mesh.shape["dp"] // nxc

    def on_device(q, k, v, o, do, lse, x, docs, tiles):
        width = x.shape[2]
        own_rows = width // (ns * nz * nxc)
        part = own_rows * nz
        rows = part * ns
        padded = -(-own_rows // 8) * 8
        slots = len(REL)
        bf, f32 = jnp.bfloat16, jnp.float32
        hbm = pl.BlockSpec(memory_space=pl.ANY)
        smem = pl.BlockSpec(memory_space=pltpu.SMEM)
        dma = pltpu.SemaphoreType.DMA
        scratch = [
            pltpu.VMEM((TOK, HQ * HEAD), bf),
            pltpu.VMEM((TOK, HQ * HEAD), bf),
            pltpu.VMEM((TOK, HQ * HEAD), bf),
            pltpu.VMEM((TOK, HQ), f32),
            pltpu.VMEM((TOK, width), bf),
            pltpu.VMEM((slots, KV, 2, TOK, HEAD), bf),
            pltpu.VMEM((slots // 2, 2 * TOK, 2 * TOK), f32),
            pltpu.VMEM((HQ, TOK), f32),
            pltpu.VMEM((TOK, HQ * HEAD), bf),
            pltpu.VMEM((KV, 2, TOK, HEAD), f32),
            pltpu.VMEM((slots - 1, KV, 2, TOK, HEAD), bf),
            pltpu.VMEM((slots - 1, KV, 2, TOK, HEAD), bf),
            pltpu.VMEM((2, TOK, KV * HEAD), bf),
            pltpu.VMEM((nz, nxc, rows // nz, TOK), bf),
            pltpu.VMEM((nxc, nz, rows // nz, TOK), bf),
            pltpu.VMEM((rows, nxc * TOK), bf),
            pltpu.VMEM((KV, nxc, TOK, HEAD), bf),
            pltpu.VMEM((KV, rows, HEAD), f32),
            pltpu.VMEM((KV, ns, part, HEAD), bf),
            pltpu.VMEM((KV, ns - 1, part, HEAD), bf),
            pltpu.VMEM((part, KV * HEAD), f32),
            pltpu.VMEM((nz, padded, KV * HEAD), f32),
            pltpu.VMEM((max(nz - 1, 1), padded, KV * HEAD), f32),
            pltpu.VMEM((own_rows, KV * HEAD), f32),
            dma((KV, 2)),
            dma((5,)),
            dma((KV + 3,)),
            dma((slots - 1, KV)),
            dma((slots - 1, KV)),
            dma((slots - 1, KV)),
            dma((slots - 1, KV)),
            dma((nxc - 1,)),
            dma((nxc - 1,)),
            dma((KV, 2 * nx - 1)),
            dma((KV, nxc)),
            dma((KV, ns - 1)),
            dma((KV, ns - 1)),
            dma((max(nz - 1, 1),)),
            dma((max(nz - 1, 1),)),
        ]
        dq, dk, dv, dw = pl.pallas_call(
            functools.partial(kernel, nx, nz, ns),
            out_shape=(
                jax.ShapeDtypeStruct((TOK, HQ * HEAD), bf),
                jax.ShapeDtypeStruct((TOK, KV * HEAD), bf),
                jax.ShapeDtypeStruct((TOK, KV * HEAD), bf),
                jax.ShapeDtypeStruct((own_rows, KV * HEAD), f32),
            ),
            in_specs=[smem, smem] + [hbm] * 7,
            out_specs=(hbm,) * 4,
            scratch_shapes=scratch,
            compiler_params=pltpu.CompilerParams(
                collective_id=0, has_side_effects=True, vmem_limit_bytes=48 * 2**20
            ),
        )(docs, tiles, q[0], k[0], v[0], o[0], do[0], lse[0], x[0])
        return dq[None], dk[None], dv[None], dw

    split = P("dp", "seq", None)
    return jax.shard_map(
        on_device,
        mesh=mesh,
        in_specs=(split,) * 7 + (P("dp", None),) * 2,
        out_specs=(split,) * 3 + (P(("dp", "seq"), None),),
        check_vma=False,
    )
```

time: 589 us -> 79.6 us (0.14)
  waiting for transfers between devices: 301 us -> 0 us
  local copies, waits for them, and re-layouts: 127 us -> 11.8 us
  matrix products: 74.9 us -> 0 us
  Pallas kernels: 0 us -> 66.2 us
  starting transfers between devices: 42.2 us -> 0 us
  between operations: 14.2 us -> 0.66 us
  blocking collectives: 13 us -> 0 us
  other arithmetic: 9.67 us -> 0 us
    unnamed x2 -> x0, waiting for transfers between devices: 249 us -> none
    dot_general x41 -> x0, matrix products: 74.9 us -> none  [the longest x8 17.6 us: tile_grads(): jnp.einsum('hgqk,qhgd->khd', scores_bf, query_tile, preferred_element_typ...]
    pallas_call x0 -> x1, Pallas kernels: none -> 66.2 us  [on_device(): pl.pallas_call(functools.partial(kernel, nx, nz, ns), out_shape=(jax.Shap...]
    all_to_all x8 -> x0, waiting for transfers between devices: 52 us -> none  [the longest x1 11 us: on_device(): lax.all_to_all(queries[0], 'seq', split_axis=1, concat_axis=0, tiled=True)]
    dynamic_slice x56 -> x0, local copies, waits for them, and re-layouts: 51.2 us -> none  [the longest x16 13.9 us: tile_grads(): lax.dynamic_slice_in_dim(value_total, col_start, col_block, 0) + value_part]
    all_to_all x8 -> x0, starting transfers between devices: 42.1 us -> none  [the longest x1 6.07 us: on_device(): lax.all_to_all(log_denominator[0], 'seq', split_axis=1, concat_axis=0, ti...]
    dynamic_update_slice x32 -> x0, local copies, waits for them, and re-layouts: 19.3 us -> none  [the longest x16 13.3 us: tile_grads(): lax.dynamic_update_slice_in_dim(key_total, lax.dynamic_slice_in_dim(key_t...]
    while x48 -> x0, local copies, waits for them, and re-layouts: 17.5 us -> none
  transfers between devices with their start and end apart: 9 -> 0, of which waited for: 8 -> 0; matrix products, arithmetic and copies ran while one was open for 6% -> 0% of each run, Pallas kernels for 0% -> 0%
where the time goes in v1:
time: 79.6 us; the launch traced here: 78.7 us
  Pallas kernels  66.2 us (83%)
  local copies, waits for them, and re-layouts  11.8 us (15%)
    pallas_call x1, Pallas kernels, on_device(): pl.pallas_call(functools.partial(kernel, nx, nz, ns), out_shape=(jax.Shap...  66.2 us
    unnamed x21, local copies, waits for them, and re-layouts  11.8 us

profile of v1, /device:TPU:32, one launch (start us, length us, event | category | flops | bytes accessed | tf_op | source)
XLA Modules:
  0.0 78.7 jit_solution(917125846894907752)
XLA Ops:
  0.6 0.8 %copy.13 = f32[1,128,32]{2,1,0:T(8,128)S(1)} copy(f32[1,128,32]{1,2,0:T(8,128)} %param.14) | data formatting | bytes 32768 | tf_op args[5]
  1.4 0.0 copy-start
  1.5 1.3 %copy-done = bf16[1,128,5120]{2,1,0:T(8,128)(2,1)S(1)} copy-done((bf16[1,128,5120]{2,1,0:T(8,128)(2,1)S(1)}, bf16[1,128,5120]{2,1,0:T(8,128)(2,1)}, u32[]{:S(2)}) %copy-start) | copy-done | bytes 1310744
  2.8 0.0 copy-start.1
  2.8 1.2 %copy-done.1 = bf16[1,128,4096]{2,1,0:T(8,128)(2,1)S(1)} copy-done((bf16[1,128,4096]{2,1,0:T(8,128)(2,1)S(1)}, bf16[1,128,4096]{2,1,0:T(8,128)(2,1)}, u32[]{:S(2)}) %copy-start.1) | copy-done | bytes 1048600
  4.0 0.0 copy-start.2
  4.0 1.2 %copy-done.2 = bf16[1,128,4096]{2,1,0:T(8,128)(2,1)S(1)} copy-done((bf16[1,128,4096]{2,1,0:T(8,128)(2,1)S(1)}, bf16[1,128,4096]{2,1,0:T(8,128)(2,1)}, u32[]{:S(2)}) %copy-start.2) | copy-done | bytes 1048600
  5.2 0.0 copy-start.3
  5.2 1.2 %copy-done.3 = bf16[1,128,4096]{2,1,0:T(8,128)(2,1)S(1)} copy-done((bf16[1,128,4096]{2,1,0:T(8,128)(2,1)S(1)}, bf16[1,128,4096]{2,1,0:T(8,128)(2,1)}, u32[]{:S(2)}) %copy-start.3) | copy-done | bytes 1048600
  6.4 0.0 copy-start.4
  6.4 0.9 %copy-done.4 = bf16[1,128,512]{2,1,0:T(8,128)(2,1)S(1)} copy-done((bf16[1,128,512]{2,1,0:T(8,128)(2,1)S(1)}, bf16[1,128,512]{2,1,0:T(8,128)(2,1)}, u32[]{:S(2)}) %copy-start.4) | copy-done | bytes 131096
  7.3 0.0 copy-start.5
  7.3 0.9 %copy-done.5 = bf16[1,128,512]{2,1,0:T(8,128)(2,1)S(1)} copy-done((bf16[1,128,512]{2,1,0:T(8,128)(2,1)S(1)}, bf16[1,128,512]{2,1,0:T(8,128)(2,1)}, u32[]{:S(2)}) %copy-start.5) | copy-done | bytes 131096
  8.3 0.0 copy-start.6
  8.3 0.7 copy-done.6
  8.9 0.0 copy-start.7
  8.9 0.7 copy-done.7
  9.6 66.2 %shard_map.120 = (bf16[128,4096]{1,0:T(8,128)(2,1)S(1)}, bf16[128,512]{1,0:T(8,128)(2,1)S(1)}, bf16[128,512]{1,0:T(8,128)(2,1)S(1)}, f32[20,512]{1,0:T(8,128)S(1)}) custom-call(s32[1,8]{1,0:T(1,128)S(1)} %copy-done.6, s32[1,8]{1,0:T(1,128)S(1)} %copy-done.7, bf16[128,4096]{1,0:T(8,128)(2,1)S(1)} %bitcast.12, bf16[128,512]{1,0:T(8,128)(2,1)S(1)} %bitcast.18, ...), custom_call_target="tpu_custom_call" | custom-call | tf_op jit(solution)/shard_map/pallas_call | solution.py:400
  75.8 1.0 %copy.18 = bf16[1,128,4096]{2,1,0:T(8,128)(2,1)} copy(bf16[1,128,4096]{2,1,0:T(8,128)(2,1)S(1)} %bitcast.11) | data formatting | bytes 2097152
  76.8 0.7 copy.19
  77.4 0.7 copy.20
  78.1 0.6 copy.21
Async XLA Ops:
  1.4 1.3 %copy-start = (bf16[1,128,5120]{2,1,0:T(8,128)(2,1)S(1)}, bf16[1,128,5120]{2,1,0:T(8,128)(2,1)}, u32[]{:S(2)}) copy-start(bf16[1,128,5120]{2,1,0:T(8,128)(2,1)} %param.15) | copy-start | bytes 3932164
  2.8 1.2 %copy-start.1 = (bf16[1,128,4096]{2,1,0:T(8,128)(2,1)S(1)}, bf16[1,128,4096]{2,1,0:T(8,128)(2,1)}, u32[]{:S(2)}) copy-start(bf16[1,128,4096]{2,1,0:T(8,128)(2,1)} %param.9) | copy-start | bytes 3145732
  4.0 1.2 %copy-start.2 = (bf16[1,128,4096]{2,1,0:T(8,128)(2,1)S(1)}, bf16[1,128,4096]{2,1,0:T(8,128)(2,1)}, u32[]{:S(2)}) copy-start(bf16[1,128,4096]{2,1,0:T(8,128)(2,1)} %param.12) | copy-start | bytes 3145732
  5.2 1.2 %copy-start.3 = (bf16[1,128,4096]{2,1,0:T(8,128)(2,1)S(1)}, bf16[1,128,4096]{2,1,0:T(8,128)(2,1)}, u32[]{:S(2)}) copy-start(bf16[1,128,4096]{2,1,0:T(8,128)(2,1)} %param.13) | copy-start | bytes 3145732
  6.4 0.9 %copy-start.4 = (bf16[1,128,512]{2,1,0:T(8,128)(2,1)S(1)}, bf16[1,128,512]{2,1,0:T(8,128)(2,1)}, u32[]{:S(2)}) copy-start(bf16[1,128,512]{2,1,0:T(8,128)(2,1)} %param.10) | copy-start | bytes 393220
  7.3 0.9 %copy-start.5 = (bf16[1,128,512]{2,1,0:T(8,128)(2,1)S(1)}, bf16[1,128,512]{2,1,0:T(8,128)(2,1)}, u32[]{:S(2)}) copy-start(bf16[1,128,512]{2,1,0:T(8,128)(2,1)} %param.11) | copy-start | bytes 393220
  8.3 0.7 copy-start.6
  8.9 0.7 copy-start.7

commit v2 on v1

v2 whole, which is shorter than its diff:
```python
import functools
import math

import jax
import jax.numpy as jnp
from jax import lax
from jax.experimental import pallas as pl
from jax.experimental.pallas import tpu as pltpu
from jax.sharding import PartitionSpec as P

HQ = 32
KV = 4
HEAD = 128
GROUP = HQ // KV
TILE_TOK = 32
TOK = 128
CORES = 2
SCALE = HEAD ** -0.5
LOG2E = math.log2(math.e)
HIDDEN = -1e30
REL = (0, 1, -1, -2, -3, -4)
NT = (((1,), (1,)), ((), ()))


def kernel(
    nx, nz, ns, doc_ref, tiles_ref, q_hbm, k_hbm, v_hbm, o_hbm, do_hbm, lse_hbm, x_hbm,
    dq_hbm, dk_hbm, dv_hbm, dw_hbm,
    q_s, o_s, do_s, x_s, kvb, bias, lse_t, delta_s, prob_s, dq_s, own, mid, sb, rb, dkv,
    x_t, xg, xp, dvall, wf, st1, r1, acc, st2, r2, out_s,
    ld_kv, ld, out_sem, kv_ss, kv_rs, pg_ss, pg_rs, x_ss, x_rs, ag_ss, ag_rs, rs_ss, rs_rs, z_ss, z_rs,
):
    nxc = nx * CORES
    d = lax.axis_index("dp")
    s = lax.axis_index("seq")
    zh = d // nxc
    i = lax.rem(d, nxc)
    xc = i // CORES
    core = lax.rem(i, CORES)
    rows = wf.shape[1]
    part = rows // ns
    own_rows = part // nz

    def remote(src, dst, ss, rs, **where):
        return pltpu.make_async_remote_copy(
            src_ref=src, dst_ref=dst, send_sem=ss, recv_sem=rs, device_id=where,
            device_id_type=pl.DeviceIdType.MESH,
        )

    def inside(t):
        return (t >= 0) & (t < ns)

    def wrap(t):
        return lax.rem(t + ns, ns)

    barrier = pltpu.get_barrier_semaphore()
    peers = [dict(seq=wrap(s + m)) for m in range(1, ns)]
    peers += [dict(dp=zh * nxc + lax.rem(i + m, nxc)) for m in range(1, nxc)]
    peers += [dict(dp=lax.rem(zh + m, nz) * nxc + i) for m in range(1, nz)]
    for peer in peers:
        pl.semaphore_signal(barrier, inc=1, device_id=peer, device_id_type=pl.DeviceIdType.MESH)

    def kv_load(g, half):
        src = (k_hbm, v_hbm)[half]
        return pltpu.make_async_copy(src.at[:, pl.ds(g * HEAD, HEAD)], kvb.at[0, g, half], ld_kv.at[g, half])

    for g in range(KV):
        kv_load(g, 0).start()
        kv_load(g, 1).start()
    loads = [
        pltpu.make_async_copy(src, dst, ld.at[n])
        for n, (src, dst) in enumerate(
            ((x_hbm, x_s), (do_hbm, do_s), (o_hbm, o_s), (q_hbm, q_s), (lse_hbm, lse_t))
        )
    ]
    for copy in loads:
        copy.start()
    for c in range(1, len(REL)):
        @pl.when(jnp.logical_not(inside(s + REL[c])))
        def _():
            kvb[c] = jnp.zeros(kvb.shape[1:], kvb.dtype)
    st2[...] = jnp.zeros(st2.shape, st2.dtype)

    z = lax.rem(s, 2)

    def kv_copy(g, n, half):
        held, slot, to, wanted = (
            (0, 2 - z, s + 1 - 2 * z, True),
            (0, 3, s + 2, True),
            (3, 5, s + 2, inside(s - 2)),
            (1 + z, 2 + 2 * z, s + 2, True),
            (2, 1, s - 2, z == 1),
            (5, 4, s - 1, (z == 1) & inside(s - 4)),
        )[n]
        copy = remote(
            kvb.at[held, g, half], kvb.at[slot, g, half], kv_ss.at[n, g, half], kv_rs.at[slot - 1, g, half],
            seq=wrap(to),
        )
        return copy, inside(to) & wanted

    def kv_send(g, n, half):
        copy, wanted = kv_copy(g, n, half)

        @pl.when(wanted)
        def _():
            copy.start()

    def kv_arrived(g, c, half):
        remote(
            kvb.at[0, g, half], kvb.at[c, g, half], kv_ss.at[0, g, half], kv_rs.at[c - 1, g, half],
            seq=wrap(s + 1),
        ).wait_recv()

    def pg_copy(g, c, half):
        to = s - 2 if c >= 4 else s + REL[c]
        copy = remote(
            sb.at[c - 1, g, half], rb.at[c - 1, g, half], pg_ss.at[c - 1, g, half], pg_rs.at[c - 1, g, half],
            seq=wrap(to),
        )
        return copy, inside(s + REL[c])

    def pg_send(g, c, half):
        copy, wanted = pg_copy(g, c, half)

        @pl.when(wanted)
        def _():
            copy.start()

    def pg_from(c):
        return inside(s + 2) & inside(s + 2 + REL[c]) if c >= 4 else inside(s - REL[c])

    loads[0].wait()
    slab = rows // nz
    for tile in range(x_s.shape[1] // TOK):
        turned = x_s[:, tile * TOK:(tile + 1) * TOK].T
        at = tile * TOK
        while at < (tile + 1) * TOK:
            block, offset = divmod(at, slab)
            length = min((tile + 1) * TOK - at, slab - offset)
            lead = at - tile * TOK
            x_t[block // nxc, block % nxc, offset:offset + length, :] = turned[lead:lead + length, :]
            at += length

    def x_copy(m):
        j = lax.rem(i + m, nxc)
        return remote(x_t.at[:, j], xg.at[i], x_ss.at[m - 1], x_rs.at[m - 1], dp=zh * nxc + j)

    xg[i] = x_t[:, i]

    row = s * TOK + lax.broadcasted_iota(jnp.int32, (1, TOK), 1)
    low = jnp.zeros((1, TOK), jnp.int32)
    high = jnp.zeros((1, TOK), jnp.int32)
    start = jnp.int32(0)
    for n in range(doc_ref.shape[1]):
        length = doc_ref[0, n]
        image_end = start + jnp.minimum(tiles_ref[0, n] * TILE_TOK, length)
        here = row >= start
        low = jnp.where(here, start, low)
        high = jnp.where(here, image_end, high)
        start = start + length
    high = jnp.maximum(row + 1, high)
    for c in range(len(REL)):
        key = (s + REL[c]) * TOK + lax.broadcasted_iota(jnp.int32, (TOK, TOK), 0)
        tile = jnp.where((key >= low) & (key < high), 0.0, HIDDEN).astype(jnp.float32)
        p, half = divmod(c, 2)
        bias[p, half * TOK:(half + 1) * TOK, :TOK] = tile
        bias[p, half * TOK:(half + 1) * TOK, TOK:] = tile
    for g in range(KV):
        kv_load(g, 0).wait()
        kv_load(g, 1).wait()
    pl.semaphore_wait(barrier, len(peers))
    def send_own(half):
        for g in range(KV):
            kv_send(g, 0, half)
            kv_send(g, 1, half)

    send_own(0)
    for m in range(1, nxc):
        x_copy(m).start()
    for copy in loads[1:]:
        copy.wait()

    head_lane = lax.broadcasted_iota(jnp.int32, (GROUP, GROUP * HEAD), 1)
    head_row = lax.broadcasted_iota(jnp.int32, (GROUP, GROUP * HEAD), 0)
    picks = ((head_lane >= head_row * HEAD) & (head_lane < (head_row + 1) * HEAD)).astype(jnp.bfloat16)

    def dq_copy(g):
        cols = pl.ds(g * GROUP * HEAD, GROUP * HEAD)
        return pltpu.make_async_copy(dq_s.at[:, cols], dq_hbm.at[:, cols], out_sem.at[g])

    def group_rows(g):
        return pl.ds(pl.multiple_of(g * GROUP, GROUP), GROUP)

    def row_delta(g, carry):
        wide = pl.ds(pl.multiple_of(g * GROUP * HEAD, GROUP * HEAD), GROUP * HEAD)
        product = do_s[:, wide].astype(jnp.float32) * o_s[:, wide].astype(jnp.float32)
        coarse = product.astype(jnp.bfloat16)
        fine = (product - coarse.astype(jnp.float32)).astype(jnp.bfloat16)
        delta = lax.dot_general(picks, coarse, NT, preferred_element_type=jnp.float32)
        delta += lax.dot_general(picks, fine, NT, preferred_element_type=jnp.float32)
        delta_s[group_rows(g), :] = delta
        return carry

    lax.fori_loop(0, KV, row_delta, 0)

    def forward(half, g):
        @pl.when(z == 0)
        def _():
            kv_arrived(g, 1, half)

        @pl.when(z == 1)
        def _():
            kv_arrived(g, 2, half)

        kv_send(g, 3, half)
        kv_send(g, 4, half)

        @pl.when(inside(s - 2))
        def _():
            kv_arrived(g, 3, half)

        kv_send(g, 2, half)

    def forward_keys(g, carry):
        forward(0, g)
        return carry

    lax.fori_loop(0, KV, forward_keys, 0)
    send_own(1)

    def heads(ref, g):
        return jnp.concatenate([ref[:, pl.ds((g * GROUP + h) * HEAD, HEAD)] for h in range(GROUP)], axis=0)

    def await_blocks(g, p, half):
        awaited = (
            ((1, z == 1),),
            ((5, z == 1), (2, z == 0)),
            ((4, z >= 0), (5, z == 0)),
        )[p]
        for c, here in awaited:
            @pl.when(inside(s + REL[c]) & here)
            def _():
                kv_arrived(g, c, half)

            if p == 1 and c == 5:
                kv_send(g, 5, half)
        return jnp.concatenate([kvb[2 * p, g, half], kvb[2 * p + 1, g, half]], axis=0)

    def keep(g, p, half, partial):
        for c in (2 * p, 2 * p + 1):
            block = partial[(c - 2 * p) * TOK:(c - 2 * p + 1) * TOK]
            if c == 0:
                own[g, half] = block
            elif c in (2, 3):
                mid[c - 2, g, half] = block
            else:
                sb[c - 1, g, half] = block.astype(jnp.bfloat16)
                pg_send(g, c, half)

    pairs = [(n, slice(n * 2 * TOK, (n + 1) * 2 * TOK)) for n in range(GROUP // 2)]

    def two_rows(stat, n):
        return jnp.concatenate([stat[2 * n:2 * n + 1], stat[2 * n + 1:2 * n + 2]], axis=1)

    def attend_values(g):
        stat = lse_t[group_rows(g), :] * LOG2E
        q8, do8 = heads(q_s, g), heads(do_s, g)
        for p in range(len(REL) // 2):
            keys = await_blocks(g, p, 0)
            probs = []
            for n, cut in pairs:
                scores = lax.dot_general(keys, q8[cut], NT, preferred_element_type=jnp.float32)
                prob = jnp.exp2(scores * (SCALE * LOG2E) - two_rows(stat, n) + bias[p])
                prob_s[g, p, :, cut] = prob
                probs.append(prob.astype(jnp.bfloat16))
            probs = jnp.concatenate(probs, axis=1)
            keep(g, p, 1, jnp.dot(probs, do8, preferred_element_type=jnp.float32))

    def attend_keys(g):
        delta = delta_s[group_rows(g), :]
        q8, do8 = heads(q_s, g), heads(do_s, g)
        total = None
        for p in range(len(REL) // 2):
            values = await_blocks(g, p, 1)
            keys = jnp.concatenate([kvb[2 * p, g, 0], kvb[2 * p + 1, g, 0]], axis=0)
            steps = []
            for n, cut in pairs:
                grad = lax.dot_general(values, do8[cut], NT, preferred_element_type=jnp.float32)
                steps.append((prob_s[g, p, :, cut] * (grad - two_rows(delta, n))).astype(jnp.bfloat16))
            steps = jnp.concatenate(steps, axis=1)
            keep(g, p, 0, jnp.dot(steps, q8, preferred_element_type=jnp.float32) * SCALE)
            dq = jnp.dot(keys.T, steps, preferred_element_type=jnp.float32)
            total = dq if total is None else total + dq
        for h in range(GROUP):
            dq_s[:, pl.ds((g * GROUP + h) * HEAD, HEAD)] = (
                total[:, h * TOK:(h + 1) * TOK].T * SCALE
            ).astype(jnp.bfloat16)
        dq_copy(g).start()

    def reorder_columns():
        old = lax.broadcasted_iota(jnp.int32, (1, rows), 1)
        new = old
        before = 0
        for n in range(1, nz * ns):
            shift = (n % ns * nz + n // ns - n) * own_rows
            new = new + jnp.where(old >= n * own_rows, shift - before, 0)
            before = shift
        order = (lax.broadcasted_iota(jnp.int32, (rows, rows), 0) == new).astype(jnp.bfloat16)
        for m in range(1, nxc):
            x_copy(m).wait_recv()

        def reorder(jj, carry):
            two = jnp.concatenate([xg[2 * jj].reshape(rows, TOK), xg[2 * jj + 1].reshape(rows, TOK)], axis=1)
            xp[:, pl.ds(pl.multiple_of(jj * 2 * TOK, 2 * TOK), 2 * TOK)] = jnp.dot(
                order, two, preferred_element_type=jnp.float32
            ).astype(jnp.bfloat16)
            return carry

        lax.fori_loop(0, nxc // 2, reorder, 0)

    def ag_copy(g, m):
        to = lax.rem(i + m, nxc)
        return remote(
            dvall.at[g, i], dvall.at[g, i], ag_ss.at[g, m - 1], ag_rs.at[g, m - 1], dp=zh * nxc + to
        )

    def group_cols(g):
        return pl.ds(pl.multiple_of(g * HEAD, HEAD), HEAD)

    def pass_on(half, g):
        for c in (4, 5):
            @pl.when(pg_from(c))
            def _():
                pg_copy(g, c, half)[0].wait_recv()
                mid[c - 4, g, half] += rb[c - 1, g, half].astype(jnp.float32)

            sb[c - 3, g, half] = mid[c - 4, g, half].astype(jnp.bfloat16)
            pg_send(g, c - 2, half)

    def settle(half, g):
        for c in (1, 2, 3):
            @pl.when(pg_from(c))
            def _():
                pg_copy(g, c, half)[0].wait_recv()
                own[g, half] += rb[c - 1, g, half].astype(jnp.float32)
        done = own[g, half].astype(jnp.bfloat16)
        dkv[half, :, group_cols(g)] = done
        if half == 1:
            dvall[g, i] = done
            for m in range(1, nxc):
                ag_copy(g, m).start()

    def rs_copy(g, m):
        to = wrap(s + m)
        return remote(st1.at[g, to], r1.at[g, m - 1], rs_ss.at[g, m - 1], rs_rs.at[g, m - 1], seq=to)

    def weight(g):
        for m in range(1, nxc):
            src = dvall.at[g, lax.rem(i - m + nxc, nxc)]
            remote(src, src, ag_ss.at[g, m - 1], ag_rs.at[g, m - 1], dp=zh * nxc + lax.rem(i + m, nxc)).wait_recv()
        values = dvall[g].reshape(nxc * TOK, HEAD)
        product = jnp.dot(xp[...], values, preferred_element_type=jnp.float32)
        wf[g] = product
        st1[g] = product.astype(jnp.bfloat16).reshape(ns, part, HEAD)
        for m in range(1, ns):
            rs_copy(g, m).start()

    def z_copy(g, m):
        to = lax.rem(zh + m, nz)
        return remote(
            st2.at[g, to], r2.at[g, m - 1], z_ss.at[g, m - 1], z_rs.at[g, m - 1], dp=to * nxc + i
        )

    def sum_seq(g):
        mine = wf[g, pl.ds(pl.multiple_of(s * part, part), part), :]
        for m in range(1, ns):
            rs_copy(g, m).wait_recv()
            mine = mine + r1[g, m - 1].astype(jnp.float32)
        acc[g] = mine
        for n in range(nz):
            st2[g, n, :own_rows, :] = acc[g, n * own_rows:(n + 1) * own_rows, :]
        for m in range(1, nz):
            z_copy(g, m).start()

    def sum_z(g):
        result = st2[g, zh, :own_rows, :]
        for m in range(1, nz):
            z_copy(g, m).wait_recv()
            result = result + r2[g, m - 1, :own_rows, :]
        out_s[:, group_cols(g)] = result * ((ns * nz * nxc * TOK) ** -0.5)

    out_k = pltpu.make_async_copy(dkv.at[0], dk_hbm, out_sem.at[KV])
    out_v = pltpu.make_async_copy(dkv.at[1], dv_hbm, out_sem.at[KV + 1])
    out_w = pltpu.make_async_copy(out_s, dw_hbm, out_sem.at[KV + 2])

    stages = (
        (attend_values, 0),
        (functools.partial(forward, 1), 0),
        (functools.partial(pass_on, 1), 1),
        (functools.partial(settle, 1), 2),
        (weight, 3),
        (sum_seq, 4),
        (attend_keys, 2),
        (functools.partial(pass_on, 0), 3),
        (functools.partial(settle, 0), 4),
    )

    def step(t, carry):
        @pl.when(t == 2)
        def _():
            reorder_columns()

        for stage, behind in stages:
            @pl.when((t >= behind) & (t < behind + KV))
            def _():
                stage(t - behind)
        return carry

    lax.fori_loop(0, KV + max(behind for _, behind in stages), step, 0)
    out_k.start()
    out_v.start()
    for g in range(KV):
        sum_z(g)
    out_w.start()

    def drain(g, carry):
        for half in range(2):
            for n in range(6):
                copy, wanted = kv_copy(g, n, half)

                @pl.when(wanted)
                def _():
                    copy.wait_send()
            for c in range(1, len(REL)):
                sent, given = pg_copy(g, c, half)

                @pl.when(given)
                def _():
                    sent.wait_send()
        for m in range(1, nxc):
            ag_copy(g, m).wait_send()
        for m in range(1, ns):
            rs_copy(g, m).wait_send()
        for m in range(1, nz):
            z_copy(g, m).wait_send()
        dq_copy(g).wait()
        return carry

    lax.fori_loop(0, KV, drain, 0)
    for m in range(1, nxc):
        x_copy(m).wait_send()
    out_k.wait()
    out_v.wait()
    out_w.wait()


def finish(*refs):
    ins, outs, held, ld, out_sem = refs[:4], refs[4:8], refs[8:12], refs[12], refs[13]
    loads, stores = [], []
    for src, dst, mid in zip(ins, outs, held):
        for col in range(0, src.shape[1], KV * HEAD):
            n, part = len(loads), (slice(None), pl.ds(col, KV * HEAD))
            loads.append(pltpu.make_async_copy(src.at[part], mid.at[part], ld.at[n]))
            stores.append(pltpu.make_async_copy(mid.at[part], dst.at[part], out_sem.at[n]))
    for copy in loads:
        copy.start()
    for copy, store in zip(loads, stores):
        copy.wait()
        store.start()
    for store in stores:
        store.wait()


def solution(mesh, nx=4):
    ns = mesh.shape["seq"]
    nxc = nx * CORES
    nz = mesh.shape["dp"] // nxc

    def on_device(q, k, v, o, do, lse, x, docs, tiles):
        width = x.shape[2]
        own_rows = width // (ns * nz * nxc)
        part = own_rows * nz
        rows = part * ns
        padded = -(-own_rows // 8) * 8
        slots = len(REL)
        bf, f32 = jnp.bfloat16, jnp.float32
        hbm = pl.BlockSpec(memory_space=pl.ANY)
        smem = pl.BlockSpec(memory_space=pltpu.SMEM)
        dma = pltpu.SemaphoreType.DMA
        scratch = [
            pltpu.VMEM((TOK, HQ * HEAD), bf),
            pltpu.VMEM((TOK, HQ * HEAD), bf),
            pltpu.VMEM((TOK, HQ * HEAD), bf),
                        pltpu.VMEM((TOK, width), bf),
            pltpu.VMEM((slots, KV, 2, TOK, HEAD), bf),
            pltpu.VMEM((slots // 2, 2 * TOK, 2 * TOK), f32),
            pltpu.VMEM((HQ, TOK), f32),
            pltpu.VMEM((HQ, TOK), f32),
            pltpu.VMEM((KV, slots // 2, 2 * TOK, GROUP * TOK), f32),
            pltpu.VMEM((TOK, HQ * HEAD), bf),
            pltpu.VMEM((KV, 2, TOK, HEAD), f32),
            pltpu.VMEM((2, KV, 2, TOK, HEAD), f32),
            pltpu.VMEM((slots - 1, KV, 2, TOK, HEAD), bf),
            pltpu.VMEM((slots - 1, KV, 2, TOK, HEAD), bf),
            pltpu.VMEM((2, TOK, KV * HEAD), bf),
            pltpu.VMEM((nz, nxc, rows // nz, TOK), bf),
            pltpu.VMEM((nxc, nz, rows // nz, TOK), bf),
            pltpu.VMEM((rows, nxc * TOK), bf),
            pltpu.VMEM((KV, nxc, TOK, HEAD), bf),
            pltpu.VMEM((KV, rows, HEAD), f32),
            pltpu.VMEM((KV, ns, part, HEAD), bf),
            pltpu.VMEM((KV, ns - 1, part, HEAD), bf),
            pltpu.VMEM((KV, part, HEAD), f32),
            pltpu.VMEM((KV, nz, padded, HEAD), f32),
            pltpu.VMEM((KV, max(nz - 1, 1), padded, HEAD), f32),
            pltpu.VMEM((own_rows, KV * HEAD), f32),
            dma((KV, 2)),
            dma((5,)),
            dma((KV + 3,)),
            dma((slots, KV, 2)),
            dma((slots - 1, KV, 2)),
            dma((slots - 1, KV, 2)),
            dma((slots - 1, KV, 2)),
            dma((nxc - 1,)),
            dma((nxc - 1,)),
            dma((KV, nxc - 1)),
            dma((KV, nxc - 1)),
            dma((KV, ns - 1)),
            dma((KV, ns - 1)),
            dma((KV, max(nz - 1, 1))),
            dma((KV, max(nz - 1, 1))),
        ]
        shapes = (
            jax.ShapeDtypeStruct((TOK, HQ * HEAD), bf),
            jax.ShapeDtypeStruct((TOK, KV * HEAD), bf),
            jax.ShapeDtypeStruct((TOK, KV * HEAD), bf),
            jax.ShapeDtypeStruct((own_rows, KV * HEAD), f32),
        )
        results = pl.pallas_call(
            functools.partial(kernel, nx, nz, ns),
            out_shape=shapes,
            in_specs=[smem, smem] + [hbm] * 7,
            out_specs=(hbm,) * 4,
            scratch_shapes=scratch,
            compiler_params=pltpu.CompilerParams(
                collective_id=0, has_side_effects=True, vmem_limit_bytes=60 * 2**20
            ),
        )(docs, tiles, q[0], k[0], v[0], o[0], do[0], lse[0].T, x[0])
        dq, dk, dv, dw = pl.pallas_call(
            finish,
            out_shape=shapes,
            in_specs=[hbm] * 4,
            out_specs=(hbm,) * 4,
            scratch_shapes=[pltpu.VMEM(a.shape, a.dtype) for a in shapes] + [dma((GROUP + 3,))] * 2,
            compiler_params=pltpu.CompilerParams(vmem_limit_bytes=60 * 2**20),
        )(*results)
        return dq[None], dk[None], dv[None], dw

    split = P("dp", "seq", None)
    return jax.shard_map(
        on_device,
        mesh=mesh,
        in_specs=(split,) * 7 + (P("dp", None),) * 2,
        out_specs=(split,) * 3 + (P(("dp", "seq"), None),),
        check_vma=False,
    )
```

time: 79.6 us -> 68.9 us (0.87)
  local copies, waits for them, and re-layouts: 11.8 us -> 0 us
  Pallas kernels: 66.2 us -> 67.8 us
    unnamed x21 -> x0, local copies, waits for them, and re-layouts: 11.8 us -> none
    pallas_call x1 -> x2, Pallas kernels: 66.2 us -> 67.8 us  [the longest x1 65.6 us: on_device(): pl.pallas_call(functools.partial(kernel, nx, nz, ns), out_shape=shapes, i...]
where the time goes in v2:
time: 68.9 us; the launch traced here: 68.5 us
  Pallas kernels  67.8 us (98%)
    pallas_call x1, Pallas kernels, on_device(): pl.pallas_call(functools.partial(kernel, nx, nz, ns), out_shape=shapes, i...  65.6 us
    pallas_call x1, Pallas kernels, on_device(): pl.pallas_call(finish, out_shape=shapes, in_specs=[hbm] * 4, out_specs=(h...  2.24 us

profile of v2, /device:TPU:32, one launch (start us, length us, event | category | flops | bytes accessed | tf_op | source)
XLA Modules:
  0.0 68.5 jit_solution(15123372912243414065)
XLA Ops:
  0.6 65.6 %shard_map.120 = (bf16[128,4096]{1,0:T(8,128)(2,1)}, bf16[128,512]{1,0:T(8,128)(2,1)}, bf16[128,512]{1,0:T(8,128)(2,1)}, f32[20,512]{1,0:T(8,128)}) custom-call(s32[1,8]{1,0:T(1,128)} %doc_ref.1, s32[1,8]{1,0:T(1,128)} %tiles_ref.1, bf16[128,4096]{1,0:T(8,128)(2,1)} %bitcast.13, bf16[128,512]{1,0:T(8,128)(2,1)} %bitcast.16, bf16[128,512]{1,0:T(8,128)(2,1)} %bitcast.17, ...), custom_call_target="tpu_custom_call" | custom-call | tf_op jit(solution)/shard_map/pallas_call | solution.py:538
  66.2 2.2 %shard_map.121 = (bf16[128,4096]{1,0:T(8,128)(2,1)}, bf16[128,512]{1,0:T(8,128)(2,1)}, bf16[128,512]{1,0:T(8,128)(2,1)}, f32[20,512]{1,0:T(8,128)}) custom-call(bf16[128,4096]{1,0:T(8,128)(2,1)} %get-tuple-element.12.refs_0_, bf16[128,512]{1,0:T(8,128)(2,1)} %get-tuple-element.13.refs_1_, bf16[128,512]{1,0:T(8,128)(2,1)} %get-tuple-element.14.refs_2_, ...), custom_call_target="tpu_custom_call" | custom-call | tf_op jit(solution)/shard_map/pallas_call | solution.py:548

commit v3 on v2

--- a/solution.py
+++ b/solution.py
@@ -111,7 +111,7 @@
         ).wait_recv()
 
     def pg_copy(g, c, half):
-        to = s - 2 if c >= 4 else s + REL[c]
+        to = s - 2 if c >= 4 and half == 0 else s + REL[c]
         copy = remote(
             sb.at[c - 1, g, half], rb.at[c - 1, g, half], pg_ss.at[c - 1, g, half], pg_rs.at[c - 1, g, half],
             seq=wrap(to),
@@ -125,8 +125,8 @@
         def _():
             copy.start()
 
-    def pg_from(c):
-        return inside(s + 2) & inside(s + 2 + REL[c]) if c >= 4 else inside(s - REL[c])
+    def pg_from(c, half):
+        return inside(s + 2) & inside(s + 2 + REL[c]) if c >= 4 and half == 0 else inside(s - REL[c])
 
     loads[0].wait()
     slab = rows // nz
@@ -200,8 +200,6 @@
         delta_s[group_rows(g), :] = delta
         return carry
 
-    lax.fori_loop(0, KV, row_delta, 0)
-
     def forward(half, g):
         @pl.when(z == 0)
         def _():
@@ -250,8 +248,8 @@
             block = partial[(c - 2 * p) * TOK:(c - 2 * p + 1) * TOK]
             if c == 0:
                 own[g, half] = block
-            elif c in (2, 3):
-                mid[c - 2, g, half] = block
+            elif c in (2, 3) and half == 0:
+                mid[c - 2, g] = block
             else:
                 sb[c - 1, g, half] = block.astype(jnp.bfloat16)
                 pg_send(g, c, half)
@@ -326,19 +324,19 @@
     def group_cols(g):
         return pl.ds(pl.multiple_of(g * HEAD, HEAD), HEAD)
 
-    def pass_on(half, g):
+    def pass_on(g):
         for c in (4, 5):
-            @pl.when(pg_from(c))
+            @pl.when(pg_from(c, 0))
             def _():
-                pg_copy(g, c, half)[0].wait_recv()
-                mid[c - 4, g, half] += rb[c - 1, g, half].astype(jnp.float32)
-
-            sb[c - 3, g, half] = mid[c - 4, g, half].astype(jnp.bfloat16)
-            pg_send(g, c - 2, half)
+                pg_copy(g, c, 0)[0].wait_recv()
+                mid[c - 4, g] += rb[c - 1, g, 0].astype(jnp.float32)
+
+            sb[c - 3, g, 0] = mid[c - 4, g].astype(jnp.bfloat16)
+            pg_send(g, c - 2, 0)
 
     def settle(half, g):
-        for c in (1, 2, 3):
-            @pl.when(pg_from(c))
+        for c in (1, 2, 3) if half == 0 else range(1, len(REL)):
+            @pl.when(pg_from(c, half))
             def _():
                 pg_copy(g, c, half)[0].wait_recv()
                 own[g, half] += rb[c - 1, g, half].astype(jnp.float32)
@@ -354,6 +352,10 @@
         return remote(st1.at[g, to], r1.at[g, m - 1], rs_ss.at[g, m - 1], rs_rs.at[g, m - 1], seq=to)
 
     def weight(g):
+        @pl.when(g == 0)
+        def _():
+            reorder_columns()
+
         for m in range(1, nxc):
             src = dvall.at[g, lax.rem(i - m + nxc, nxc)]
             remote(src, src, ag_ss.at[g, m - 1], ag_rs.at[g, m - 1], dp=zh * nxc + lax.rem(i + m, nxc)).wait_recv()
@@ -394,20 +396,19 @@
 
     stages = (
         (attend_values, 0),
-        (functools.partial(forward, 1), 0),
-        (functools.partial(pass_on, 1), 1),
-        (functools.partial(settle, 1), 2),
-        (weight, 3),
-        (sum_seq, 4),
+        (functools.partial(settle, 1), 1),
+        (functools.partial(forward, 1), 1),
+        (weight, 2),
+        (sum_seq, 3),
         (attend_keys, 2),
-        (functools.partial(pass_on, 0), 3),
+        (pass_on, 3),
         (functools.partial(settle, 0), 4),
     )
 
     def step(t, carry):
-        @pl.when(t == 2)
-        def _():
-            reorder_columns()
+        @pl.when(t == 1)
+        def _():
+            lax.fori_loop(0, KV, row_delta, 0)
 
         for stage, behind in stages:
             @pl.when((t >= behind) & (t < behind + KV))
@@ -498,7 +499,7 @@
             pltpu.VMEM((KV, slots // 2, 2 * TOK, GROUP * TOK), f32),
             pltpu.VMEM((TOK, HQ * HEAD), bf),
             pltpu.VMEM((KV, 2, TOK, HEAD), f32),
-            pltpu.VMEM((2, KV, 2, TOK, HEAD), f32),
+            pltpu.VMEM((2, KV, TOK, HEAD), f32),
             pltpu.VMEM((slots - 1, KV, 2, TOK, HEAD), bf),
             pltpu.VMEM((slots - 1, KV, 2, TOK, HEAD), bf),
             pltpu.VMEM((2, TOK, KV * HEAD), bf),

time: 68.9 us -> 66 us (0.958)
  Pallas kernels: 67.8 us -> 65.2 us
    pallas_call x1, Pallas kernels: 65.6 us -> 63 us  [on_device(): pl.pallas_call(functools.partial(kernel, nx, nz, ns), out_shape=shapes, i...]
where the time goes in v3:
time: 66 us; the launch traced here: 65.9 us
  Pallas kernels  65.2 us (99%)
    pallas_call x1, Pallas kernels, on_device(): pl.pallas_call(functools.partial(kernel, nx, nz, ns), out_shape=shapes, i...  63 us
    pallas_call x1, Pallas kernels, on_device(): pl.pallas_call(finish, out_shape=shapes, in_specs=[hbm] * 4, out_specs=(h...  2.24 us

profile of v3, /device:TPU:32, one launch (start us, length us, event | category | flops | bytes accessed | tf_op | source)
XLA Modules:
  0.0 65.9 jit_solution(15224042592897406794)
XLA Ops:
  0.6 63.0 %shard_map.120 = (bf16[128,4096]{1,0:T(8,128)(2,1)}, bf16[128,512]{1,0:T(8,128)(2,1)}, bf16[128,512]{1,0:T(8,128)(2,1)}, f32[20,512]{1,0:T(8,128)}) custom-call(s32[1,8]{1,0:T(1,128)} %doc_ref.1, s32[1,8]{1,0:T(1,128)} %tiles_ref.1, bf16[128,4096]{1,0:T(8,128)(2,1)} %bitcast.13, bf16[128,512]{1,0:T(8,128)(2,1)} %bitcast.16, bf16[128,512]{1,0:T(8,128)(2,1)} %bitcast.17, ...), custom_call_target="tpu_custom_call" | custom-call | tf_op jit(solution)/shard_map/pallas_call | solution.py:539
  63.6 2.2 %shard_map.121 = (bf16[128,4096]{1,0:T(8,128)(2,1)}, bf16[128,512]{1,0:T(8,128)(2,1)}, bf16[128,512]{1,0:T(8,128)(2,1)}, f32[20,512]{1,0:T(8,128)}) custom-call(bf16[128,4096]{1,0:T(8,128)(2,1)} %get-tuple-element.12.refs_0_, bf16[128,512]{1,0:T(8,128)(2,1)} %get-tuple-element.13.refs_1_, bf16[128,512]{1,0:T(8,128)(2,1)} %get-tuple-element.14.refs_2_, ...), custom_call_target="tpu_custom_call" | custom-call | tf_op jit(solution)/shard_map/pallas_call | solution.py:549

commit v4 on v3

--- a/solution.py
+++ b/solution.py
@@ -20,6 +20,10 @@
 HIDDEN = -1e30
 REL = (0, 1, -1, -2, -3, -4)
 NT = (((1,), (1,)), ((), ()))
+
+
+def far_first(n):
+    return sorted(range(1, n), key=lambda m: abs(2 * m - n))
 
 
 def kernel(
@@ -174,7 +178,7 @@
             kv_send(g, 1, half)
 
     send_own(0)
-    for m in range(1, nxc):
+    for m in far_first(nxc):
         x_copy(m).start()
     for copy in loads[1:]:
         copy.wait()
@@ -344,7 +348,7 @@
         dkv[half, :, group_cols(g)] = done
         if half == 1:
             dvall[g, i] = done
-            for m in range(1, nxc):
+            for m in far_first(nxc):
                 ag_copy(g, m).start()
 
     def rs_copy(g, m):
@@ -363,7 +367,7 @@
         product = jnp.dot(xp[...], values, preferred_element_type=jnp.float32)
         wf[g] = product
         st1[g] = product.astype(jnp.bfloat16).reshape(ns, part, HEAD)
-        for m in range(1, ns):
+        for m in far_first(ns):
             rs_copy(g, m).start()
 
     def z_copy(g, m):
@@ -380,7 +384,7 @@
         acc[g] = mine
         for n in range(nz):
             st2[g, n, :own_rows, :] = acc[g, n * own_rows:(n + 1) * own_rows, :]
-        for m in range(1, nz):
+        for m in far_first(nz):
             z_copy(g, m).start()
 
     def sum_z(g):

time: 66 us -> 65.6 us (level)
  no operation moved by 1% of the time
where the time goes in v4:
time: 65.6 us; the launch traced here: 65.2 us
  Pallas kernels  64.6 us (98%)
    pallas_call x1, Pallas kernels, on_device(): pl.pallas_call(functools.partial(kernel, nx, nz, ns), out_shape=shapes, i...  62.3 us
    pallas_call x1, Pallas kernels, on_device(): pl.pallas_call(finish, out_shape=shapes, in_specs=[hbm] * 4, out_specs=(h...  2.24 us

profile of v4, /device:TPU:32, one launch (start us, length us, event | category | flops | bytes accessed | tf_op | source)
XLA Modules:
  0.0 65.2 jit_solution(7624036338631563223)
XLA Ops:
  0.6 62.3 %shard_map.120 = (bf16[128,4096]{1,0:T(8,128)(2,1)}, bf16[128,512]{1,0:T(8,128)(2,1)}, bf16[128,512]{1,0:T(8,128)(2,1)}, f32[20,512]{1,0:T(8,128)}) custom-call(s32[1,8]{1,0:T(1,128)} %doc_ref.1, s32[1,8]{1,0:T(1,128)} %tiles_ref.1, bf16[128,4096]{1,0:T(8,128)(2,1)} %bitcast.13, bf16[128,512]{1,0:T(8,128)(2,1)} %bitcast.16, bf16[128,512]{1,0:T(8,128)(2,1)} %bitcast.17, ...), custom_call_target="tpu_custom_call" | custom-call | tf_op jit(solution)/shard_map/pallas_call | solution.py:543
  63.0 2.2 %shard_map.121 = (bf16[128,4096]{1,0:T(8,128)(2,1)}, bf16[128,512]{1,0:T(8,128)(2,1)}, bf16[128,512]{1,0:T(8,128)(2,1)}, f32[20,512]{1,0:T(8,128)}) custom-call(bf16[128,4096]{1,0:T(8,128)(2,1)} %get-tuple-element.12.refs_0_, bf16[128,512]{1,0:T(8,128)(2,1)} %get-tuple-element.13.refs_1_, bf16[128,512]{1,0:T(8,128)(2,1)} %get-tuple-element.14.refs_2_, ...), custom_call_target="tpu_custom_call" | custom-call | tf_op jit(solution)/shard_map/pallas_call | solution.py:553
